TPU v7x, 256 devices: a whole 4x4x8 slice. The times are simulated.
256 devices in a mesh: dp: 32 (over y, x, core), tensor: 8 (over z).
Axes of the slice: x: 4, y: 4, z: 8, core: 2. Of those that a mesh axis runs over, the one named last changes fastest.
Arguments:
- query_input: bfloat16 [32768, 8192], P(('dp', 'tensor')), may hold values from -150 to 150
- key_input: bfloat16 [32768, 1024], P(('dp', 'tensor')), may hold values from -6 to 6
- value_input: bfloat16 [32768, 1024], P(('dp', 'tensor')), may hold values from -6 to 6
- output_gradient: bfloat16 [32768, 8192], P(('dp', 'tensor')), may hold values from -6 to 6
- document_lengths: int32 [32, 8], replicated, may hold values from 1 to 1017, as said below
Outputs:
- attn_out: bfloat16 [32768, 8192], P(('dp', 'tensor'))
- query_grad: bfloat16 [32768, 8192], P(('dp', 'tensor'))
- key_grad: bfloat16 [32768, 1024], P(('dp', 'tensor'))
- value_grad: bfloat16 [32768, 1024], P(('dp', 'tensor'))
Inputs may be any that keep to these rules, and one draw needn't show every extreme that they name: `document_lengths`: each pack's 8 lengths sum to 1024.
All inputs are finite; a program needn't handle non-finite values.
Results may differ from a plain program's by a relative error of at most 0.03.
Values may be sent and summed in bfloat16 or wider, within the bound.
A program may use at most 128 MiB of HBM per device.

v0:
```python
import math

import jax
import jax.numpy as jnp
from jax import lax
from jax.sharding import PartitionSpec as P

KEY_VALUE_HEADS = 8


NEGATIVE = -1e30


def swapped(x, axis, distance):
    return lax.ppermute(x, axis, [(i, i ^ 1 << distance) for i in range(lax.axis_size(axis))])


def document_index(lengths, positions):
    doc_ends = jnp.cumsum(lengths)
    return jnp.sum((positions[:, None] >= doc_ends[None, :]).astype(jnp.int32), axis=1)


def allowed_mask(lengths, query_pos, key_count):
    key_pos = jnp.arange(key_count, dtype=jnp.int32)
    query_doc = document_index(lengths, query_pos)
    key_doc = document_index(lengths, key_pos)
    return (query_doc[:, None] == key_doc[None, :]) & (key_pos[None, :] <= query_pos[:, None])


def attend(query_rows, current_keys, current_values, current_gradients, allowed, groups):
    row_count = query_rows.shape[0]
    key_count = current_keys.shape[0]
    head_dim = current_keys.shape[1] // groups
    repeat_count = query_rows.shape[1] // (groups * head_dim)
    scaling = 1.0 / math.sqrt(head_dim)
    grouped_queries = query_rows.reshape(row_count, groups, repeat_count, head_dim).transpose(
        1, 2, 0, 3
    )
    grouped_gradient = current_gradients.reshape(
        row_count, groups, repeat_count, head_dim
    ).transpose(1, 2, 0, 3)
    grouped_keys = current_keys.reshape(key_count, groups, head_dim).transpose(1, 0, 2)
    grouped_values = current_values.reshape(key_count, groups, head_dim).transpose(1, 0, 2)

    def one_group(pieces):
        query_part, key_part, value_part, grad_part = pieces
        scores = (
            jnp.einsum("gqd,kd->gqk", query_part, key_part, preferred_element_type=jnp.float32)
            * scaling
        )
        scores = jnp.where(allowed[None, :, :], scores, NEGATIVE)
        row_max = jnp.max(scores, axis=-1, keepdims=True)
        weights = jnp.exp(scores - row_max)
        attn_probs = weights / jnp.sum(weights, axis=-1, keepdims=True)
        probs_low = attn_probs.astype(jnp.bfloat16)
        attention_fn = jnp.einsum(
            "gqk,kd->gqd", probs_low, value_part, preferred_element_type=jnp.float32
        ).astype(jnp.bfloat16)
        dprobs = jnp.einsum(
            "gqd,kd->gqk", grad_part, value_part, preferred_element_type=jnp.float32
        )
        row_delta = jnp.sum(
            grad_part.astype(jnp.float32) * attention_fn.astype(jnp.float32), axis=-1, keepdims=True
        )
        dscore = (attn_probs * (dprobs - row_delta)).astype(jnp.bfloat16)
        query_gradient = (
            jnp.einsum("gqk,kd->gqd", dscore, key_part, preferred_element_type=jnp.float32)
            * scaling
        ).astype(jnp.bfloat16)
        key_term = (
            jnp.einsum("gqk,gqd->kd", dscore, query_part, preferred_element_type=jnp.float32)
            * scaling
        )
        value_term = jnp.einsum(
            "gqk,gqd->kd", probs_low, grad_part, preferred_element_type=jnp.float32
        )
        return (attention_fn, query_gradient, key_term, value_term)

    attention_fn, query_gradient, key_term, value_term = lax.map(
        one_group, (grouped_queries, grouped_keys, grouped_values, grouped_gradient)
    )
    attention_fn = attention_fn.transpose(2, 0, 1, 3).reshape(
        row_count, groups * repeat_count * head_dim
    )
    query_gradient = query_gradient.transpose(2, 0, 1, 3).reshape(
        row_count, groups * repeat_count * head_dim
    )
    key_term = key_term.transpose(1, 0, 2).reshape(key_count, groups * head_dim)
    value_term = value_term.transpose(1, 0, 2).reshape(key_count, groups * head_dim)
    return (attention_fn, query_gradient, key_term, value_term)


def body(query_input, key_input, value_input, output_gradient, document_lengths):
    row_count = query_input.shape[0]
    tensor_count = lax.axis_size("tensor")
    rows_per_pack = row_count * tensor_count
    dp_count = lax.axis_size("dp")
    group_halves = KEY_VALUE_HEADS // 2
    query_split = query_input.shape[1] // 2
    key_split = key_input.shape[1] // 2
    query_pos = lax.axis_index("tensor") * row_count + jnp.arange(row_count, dtype=jnp.int32)
    own_slot = lax.axis_index("dp")
    own_lengths = lax.dynamic_index_in_dim(document_lengths, own_slot, 0, keepdims=False)
    own_mask = allowed_mask(own_lengths, query_pos, rows_per_pack)
    flip_bit = dp_count.bit_length() - 2
    partner_slot = jnp.bitwise_xor(own_slot, 1 << flip_bit)
    partner_lengths = lax.dynamic_index_in_dim(document_lengths, partner_slot, 0, keepdims=False)
    partner_mask = allowed_mask(partner_lengths, query_pos, rows_per_pack)
    keys_all, values_all = (
        lax.all_gather(key_input, "tensor", axis=0, tiled=True),
        lax.all_gather(value_input, "tensor", axis=0, tiled=True),
    )
    arrived = swapped(
        (
            query_input[:, query_split:],
            output_gradient[:, query_split:],
            keys_all[:, key_split:],
            values_all[:, key_split:],
        ),
        "dp",
        flip_bit,
    )
    helped = attend(arrived[0], arrived[2], arrived[3], arrived[1], partner_mask, group_halves)
    returned = swapped(
        (helped[0], helped[1], helped[2].astype(jnp.bfloat16), helped[3].astype(jnp.bfloat16)),
        "dp",
        flip_bit,
    )
    kept_work = attend(
        query_input[:, :query_split],
        keys_all[:, :key_split],
        values_all[:, :key_split],
        output_gradient[:, :query_split],
        own_mask,
        group_halves,
    )
    key_terms = jnp.concatenate([kept_work[2], returned[2].astype(jnp.float32)], axis=1)
    value_terms = jnp.concatenate([kept_work[3], returned[3].astype(jnp.float32)], axis=1)
    key_sum, value_sum = (
        lax.psum_scatter(
            key_terms.astype(jnp.bfloat16), "tensor", scatter_dimension=0, tiled=True
        ).astype(jnp.float32),
        lax.psum_scatter(
            value_terms.astype(jnp.bfloat16), "tensor", scatter_dimension=0, tiled=True
        ).astype(jnp.float32),
    )
    attention_fn = jnp.concatenate([kept_work[0], returned[0]], axis=1)
    query_gradient = jnp.concatenate([kept_work[1], returned[1]], axis=1)
    key_grad = key_sum.astype(jnp.bfloat16)
    value_grad = value_sum.astype(jnp.bfloat16)
    return (attention_fn, query_gradient, key_grad, value_grad)


def solution(mesh):
    return jax.shard_map(
        body,
        mesh=mesh,
        in_specs=(
            P(("dp", "tensor"), None),
            P(("dp", "tensor"), None),
            P(("dp", "tensor"), None),
            P(("dp", "tensor"), None),
            P(),
        ),
        out_specs=(
            P(("dp", "tensor"), None),
            P(("dp", "tensor"), None),
            P(("dp", "tensor"), None),
            P(("dp", "tensor"), None),
        ),
        check_vma=False,
    )
```

profile of v0, /device:TPU:6, one launch (start us, length us, event | category | flops | bytes accessed | tf_op | source)
XLA Modules:
  0.0 363.1 jit_solution(10446641876643169491)
XLA Ops:
  12.8 3.2 collective-permute-start
  18.1 35.9 %all-gather.5.cloned.1.call-done = bf16[1024,1024]{1,0:T(8,128)(2,1)} async-done(((bf16[128,1024]{1,0:T(8,128)(2,1)}), bf16[1024,1024]{1,0:T(8,128)(2,1)}) %all-gather.5.cloned.1.call-update) | async-done | bytes 2097168 | tf_op jit(solution)/shard_map/all_gather | solution.py:111
  53.9 3.1 fusion.139
  57.0 3.1 collective-permute-start.2
  60.1 41.6 %all-gather.3.cloned.1.call-done = bf16[1024,1024]{0,1:T(8,128)(2,1)} async-done(((bf16[128,1024]{0,1:T(8,128)(2,1)}), bf16[1024,1024]{0,1:T(8,128)(2,1)}) %all-gather.3.cloned.1.call-update) | async-done | bytes 2097168 | tf_op jit(solution)/shard_map/all_gather | solution.py:110
  101.7 3.0 fusion.140
  104.8 3.0 collective-permute-start.1
  116.1 12.1 %collective-permute-done.1 = bf16[1024,512]{0,1:T(8,128)(2,1)} collective-permute-done((bf16[1024,512]{0,1:T(8,128)(2,1)}, bf16[1024,512]{0,1:T(8,128)(2,1)}, u32[]{:S(2)}, u32[]{:S(2)}) %collective-permute-start.1) | collective-permute-done | bytes 1048608 | tf_op jit(solution)/shard_map/ppermute | solution.py:15
  132.9 65.5 %while.35 = (s32[]{:T(128)}, bf16[4,8,128,128]{2,3,1,0:T(8,128)(2,1)}, bf16[4,8,128,128]{3,2,1,0:T(8,128)(2,1)}, bf16[4,1024,128]{2,1,0:T(8,128)(2,1)}, bf16[4,1...) while((s32[]{:T(128)}, ...), condition=%wide.region_15.16_spmd.clone, body=%wide.region_11.15_spmd.clone.sunk | while | flops 1622540288 | bytes 59276528 | solution.py:79
  133.1 4.5 %fusion.217 = (f32[8,128]{1,0:T(8,128)S(1)}, f32[8,128,1024]{2,1,0:T(8,128)}) fusion(pred[128,1024]{1,0:T(8,128)(4,1)S(1)} %fusion.216, bf16[4,1024,128]{1,2,0:T(8,128)(2,1)} %get-tuple-element.514, s32[]{:T(128)} %get-tuple-element.495, bf16[4,8,128,128]{2,3,1,0:T(8,128)(2,1)} %get-tuple-element.513), kind=kOutput, calls=%fused_computation.138.clone.1 | convolution fusion | flops 272630784 | bytes 4854784 | tf_op jit(solution)/shard_map/while/body/eval_jaxpr/sub | solution.py:53
  149.4 4.5 %fusion.217 = (f32[8,128]{1,0:T(8,128)S(1)}, f32[8,128,1024]{2,1,0:T(8,128)}) fusion(pred[128,1024]{1,0:T(8,128)(4,1)S(1)} %fusion.216, bf16[4,1024,128]{1,2,0:T(8,128)(2,1)} %get-tuple-element.514, s32[]{:T(128)} %get-tuple-element.495, bf16[4,8,128,128]{2,3,1,0:T(8,128)(2,1)} %get-tuple-element.513), kind=kOutput, calls=%fused_computation.138.clone.1 | convolution fusion | flops 272630784 | bytes 4854784 | tf_op jit(solution)/shard_map/while/body/eval_jaxpr/sub | solution.py:53
  165.8 4.5 %fusion.217 = (f32[8,128]{1,0:T(8,128)S(1)}, f32[8,128,1024]{2,1,0:T(8,128)}) fusion(pred[128,1024]{1,0:T(8,128)(4,1)S(1)} %fusion.216, bf16[4,1024,128]{1,2,0:T(8,128)(2,1)} %get-tuple-element.514, s32[]{:T(128)} %get-tuple-element.495, bf16[4,8,128,128]{2,3,1,0:T(8,128)(2,1)} %get-tuple-element.513), kind=kOutput, calls=%fused_computation.138.clone.1 | convolution fusion | flops 272630784 | bytes 4854784 | tf_op jit(solution)/shard_map/while/body/eval_jaxpr/sub | solution.py:53
  182.2 4.5 %fusion.217 = (f32[8,128]{1,0:T(8,128)S(1)}, f32[8,128,1024]{2,1,0:T(8,128)}) fusion(pred[128,1024]{1,0:T(8,128)(4,1)S(1)} %fusion.216, bf16[4,1024,128]{1,2,0:T(8,128)(2,1)} %get-tuple-element.514, s32[]{:T(128)} %get-tuple-element.495, bf16[4,8,128,128]{2,3,1,0:T(8,128)(2,1)} %get-tuple-element.513), kind=kOutput, calls=%fused_computation.138.clone.1 | convolution fusion | flops 272630784 | bytes 4854784 | tf_op jit(solution)/shard_map/while/body/eval_jaxpr/sub | solution.py:53
  200.7 3.0 collective-permute-start.6
  208.4 61.3 %while.34 = (s32[]{:T(128)}, bf16[4,8,128,128]{2,3,1,0:T(8,128)(2,1)}, bf16[4,8,128,128]{3,2,1,0:T(8,128)(2,1)}, bf16[4,1024,128]{2,1,0:T(8,128)(2,1)}, bf16[4,1...) while((s32[]{:T(128)}, ...), condition=%wide.region_7.8_spmd.clone, body=%wide.region_3.0_spmd.clone.sunk | while | flops 1622540288 | bytes 55082196 | solution.py:79
  208.7 4.5 %fusion.200 = (f32[8,128]{1,0:T(8,128)S(1)}, f32[8,128,1024]{2,1,0:T(8,128)}) fusion(pred[128,1024]{1,0:T(8,128)(4,1)S(1)} %fusion.199, bf16[4,1024,128]{1,2,0:T(8,128)(2,1)} %get-tuple-element.553, s32[]{:T(128)} %get-tuple-element.534, bf16[4,8,128,128]{2,3,1,0:T(8,128)(2,1)S(1)} %get-tuple-element.552), kind=kOutput, calls=%fused_computation.137.clone.1 | convolution fusion | flops 272630784 | bytes 4854784 | tf_op jit(solution)/shard_map/while/body/eval_jaxpr/sub | solution.py:53
  224.0 4.5 %fusion.200 = (f32[8,128]{1,0:T(8,128)S(1)}, f32[8,128,1024]{2,1,0:T(8,128)}) fusion(pred[128,1024]{1,0:T(8,128)(4,1)S(1)} %fusion.199, bf16[4,1024,128]{1,2,0:T(8,128)(2,1)} %get-tuple-element.553, s32[]{:T(128)} %get-tuple-element.534, bf16[4,8,128,128]{2,3,1,0:T(8,128)(2,1)S(1)} %get-tuple-element.552), kind=kOutput, calls=%fused_computation.137.clone.1 | convolution fusion | flops 272630784 | bytes 4854784 | tf_op jit(solution)/shard_map/while/body/eval_jaxpr/sub | solution.py:53
  239.3 4.5 %fusion.200 = (f32[8,128]{1,0:T(8,128)S(1)}, f32[8,128,1024]{2,1,0:T(8,128)}) fusion(pred[128,1024]{1,0:T(8,128)(4,1)S(1)} %fusion.199, bf16[4,1024,128]{1,2,0:T(8,128)(2,1)} %get-tuple-element.553, s32[]{:T(128)} %get-tuple-element.534, bf16[4,8,128,128]{2,3,1,0:T(8,128)(2,1)S(1)} %get-tuple-element.552), kind=kOutput, calls=%fused_computation.137.clone.1 | convolution fusion | flops 272630784 | bytes 4854784 | tf_op jit(solution)/shard_map/while/body/eval_jaxpr/sub | solution.py:53
  254.6 4.5 %fusion.200 = (f32[8,128]{1,0:T(8,128)S(1)}, f32[8,128,1024]{2,1,0:T(8,128)}) fusion(pred[128,1024]{1,0:T(8,128)(4,1)S(1)} %fusion.199, bf16[4,1024,128]{1,2,0:T(8,128)(2,1)} %get-tuple-element.553, s32[]{:T(128)} %get-tuple-element.534, bf16[4,8,128,128]{2,3,1,0:T(8,128)(2,1)S(1)} %get-tuple-element.552), kind=kOutput, calls=%fused_computation.137.clone.1 | convolution fusion | flops 272630784 | bytes 4854784 | tf_op jit(solution)/shard_map/while/body/eval_jaxpr/sub | solution.py:53
  277.3 20.0 %collective-permute-done.7 = bf16[1024,512]{1,0:T(8,128)(2,1)S(1)} collective-permute-done((bf16[1024,512]{1,0:T(8,128)(2,1)S(1)}, bf16[1024,512]{1,0:T(8,128)(2,1)S(1)}, u32[]{:S(2)}, u32[]{:S(2)}) %collective-permute-start.7) | collective-permute-done | bytes 1048608 | tf_op jit(solution)/shard_map/ppermute | solution.py:15
  304.1 3.0 collective-permute-start.4
  308.9 21.3 %collective-permute-done.5 = bf16[128,4096]{1,0:T(8,128)(2,1)} collective-permute-done((bf16[128,4096]{1,0:T(8,128)(2,1)}, bf16[128,4096]{1,0:T(8,128)(2,1)}, u32[]{:S(2)}, u32[]{:S(2)}) %collective-permute-start.5) | collective-permute-done | bytes 1048608 | tf_op jit(solution)/shard_map/ppermute | solution.py:15
  332.9 13.1 %collective-permute-done.4 = bf16[128,4096]{1,0:T(8,128)(2,1)} collective-permute-done((bf16[128,4096]{1,0:T(8,128)(2,1)}, bf16[128,4096]{1,0:T(8,128)(2,1)}, u32[]{:S(2)}, u32[]{:S(2)}) %collective-permute-start.4) | collective-permute-done | bytes 1048608 | tf_op jit(solution)/shard_map/ppermute | solution.py:15
  348.8 7.8 %reduce-scatter.5.cloned.1.call-done = bf16[128,1024]{1,0:T(8,128)(2,1)} async-done(((bf16[1024,1024]{1,0:T(8,128)(2,1)}), bf16[128,1024]{1,0:T(8,128)(2,1)}) %reduce-scatter.5.cloned.1.call-update) | async-done | bytes 262160 | tf_op jit(solution)/shard_map/reduce_scatter | solution.py:143
  (186 shorter events, 139.5 us)
Async XLA Ops:
  7.2 46.8 %all-gather.5.cloned.1.call-start = ((), (), s32[]{:S(2)}) async-start(), calls=%async_computation.3 | async-start | bytes 2359296 | tf_op jit(solution)/shard_map/all_gather | solution.py:111
  7.9 93.8 %all-gather.3.cloned.1.call-start = ((), (), s32[]{:S(2)}) async-start(), calls=%async_computation.2 | async-start | bytes 2359296 | tf_op jit(solution)/shard_map/all_gather | solution.py:110
  9.8 339.0 %reduce-scatter.3.cloned.1.call-start = ((), (), s32[]{:S(2)}) async-start(), calls=%async_computation.4 | async-start | bytes 2359296 | tf_op jit(solution)/shard_map/reduce_scatter | solution.py:140
  12.8 103.3 %collective-permute-start = (bf16[128,4096]{0,1:T(8,128)(2,1)}, bf16[128,4096]{0,1:T(8,128)(2,1)}, u32[]{:S(2)}, u32[]{:S(2)}) collective-permute-start(bf16[128,4096]{0,1:T(8,128)(2,1)} %copy.114), channel_id=1, source_target_pairs={{0,128},{8,136},{16,144},{24,152},{32,160},{40,168},{48,176},{56,1... | collective-permute-start | bytes 3145736 | tf_op jit(solution)/shard_map/ppermute | solution.py:15
  17.7 92.9 %collective-permute-start.3 = (bf16[128,4096]{1,0:T(8,128)(2,1)S(1)}, bf16[128,4096]{1,0:T(8,128)(2,1)}, u32[]{:S(2)}, u32[]{:S(2)}) collective-permute-start(bf16[128,4096]{1,0:T(8,128)(2,1)S(1)} %get-tuple-element.313), channel_id=1, source_target_pairs={{0,128},{8,136},{16,144},{24,152},{32,160},{40,168},{48,176},{56,1... | collective-permute-start | bytes 3145736 | tf_op jit(solution)/shard_map/ppermute | solution.py:15
  57.0 50.8 %copy-start.12 = (s32[32,8]{0,1:T(8,128)S(1)}, s32[32,8]{0,1:T(8,128)}, u32[]{:S(2)}) copy-start(s32[32,8]{0,1:T(8,128)} %param.13) | copy-start | bytes 3076
  57.0 56.7 %collective-permute-start.2 = (bf16[1024,512]{1,0:T(8,128)(2,1)}, bf16[1024,512]{1,0:T(8,128)(2,1)}, u32[]{:S(2)}, u32[]{:S(2)}) collective-permute-start(bf16[1024,512]{1,0:T(8,128)(2,1)} %get-tuple-element.315), channel_id=1, source_target_pairs={{0,128},{8,136},{16,144},{24,152},{32,160},{40,168},{48,176},{56,1... | collective-permute-start | bytes 3145736 | tf_op jit(solution)/shard_map/ppermute | solution.py:15
  104.8 23.4 %collective-permute-start.1 = (bf16[1024,512]{0,1:T(8,128)(2,1)}, bf16[1024,512]{0,1:T(8,128)(2,1)}, u32[]{:S(2)}, u32[]{:S(2)}) collective-permute-start(bf16[1024,512]{0,1:T(8,128)(2,1)} %get-tuple-element.317), channel_id=1, source_target_pairs={{0,128},{8,136},{16,144},{24,152},{32,160},{40,168},{48,176},{56,1... | collective-permute-start | bytes 3145736 | tf_op jit(solution)/shard_map/ppermute | solution.py:15
  137.6 4.5 %copy-start = (f32[8,128,1024]{2,1,0:T(8,128)S(1)}, f32[8,128,1024]{2,1,0:T(8,128)}, u32[]{:S(2)}) copy-start(f32[8,128,1024]{2,1,0:T(8,128)} %get-tuple-element.478) | copy-start | bytes 12582916 | tf_op jit(solution)/shard_map/while
  154.0 4.5 %copy-start = (f32[8,128,1024]{2,1,0:T(8,128)S(1)}, f32[8,128,1024]{2,1,0:T(8,128)}, u32[]{:S(2)}) copy-start(f32[8,128,1024]{2,1,0:T(8,128)} %get-tuple-element.478) | copy-start | bytes 12582916 | tf_op jit(solution)/shard_map/while
  170.4 4.5 %copy-start = (f32[8,128,1024]{2,1,0:T(8,128)S(1)}, f32[8,128,1024]{2,1,0:T(8,128)}, u32[]{:S(2)}) copy-start(f32[8,128,1024]{2,1,0:T(8,128)} %get-tuple-element.478) | copy-start | bytes 12582916 | tf_op jit(solution)/shard_map/while
  186.7 2.9 copy-start.2
  186.7 4.5 %copy-start = (f32[8,128,1024]{2,1,0:T(8,128)S(1)}, f32[8,128,1024]{2,1,0:T(8,128)}, u32[]{:S(2)}) copy-start(f32[8,128,1024]{2,1,0:T(8,128)} %get-tuple-element.478) | copy-start | bytes 12582916 | tf_op jit(solution)/shard_map/while
  200.7 70.4 %collective-permute-start.6 = (bf16[1024,512]{1,0:T(8,128)(2,1)}, bf16[1024,512]{1,0:T(8,128)(2,1)}, u32[]{:S(2)}, u32[]{:S(2)}) collective-permute-start(bf16[1024,512]{1,0:T(8,128)(2,1)} %copy_bitcast_fusion.4), channel_id=1, source_target_pairs={{0,128},{8,136},{16,144},{24,152},{32,160},{40,168},{48,176},{56,1... | collective-permute-start | bytes 3145736 | tf_op jit(solution)/shard_map/ppermute | solution.py:15
  203.7 4.7 %copy-start.3 = (bf16[128,4096]{0,1:T(8,128)(2,1)S(1)}, bf16[128,4096]{0,1:T(8,128)(2,1)}, u32[]{:S(2)}) copy-start(bf16[128,4096]{0,1:T(8,128)(2,1)} %copy.113) | copy-start | bytes 3145732
  213.1 4.5 %copy-start.1 = (f32[8,128,1024]{2,1,0:T(8,128)S(1)}, f32[8,128,1024]{2,1,0:T(8,128)}, u32[]{:S(2)}) copy-start(f32[8,128,1024]{2,1,0:T(8,128)} %get-tuple-element.462) | copy-start | bytes 12582916 | tf_op jit(solution)/shard_map/while
  228.4 4.5 %copy-start.1 = (f32[8,128,1024]{2,1,0:T(8,128)S(1)}, f32[8,128,1024]{2,1,0:T(8,128)}, u32[]{:S(2)}) copy-start(f32[8,128,1024]{2,1,0:T(8,128)} %get-tuple-element.462) | copy-start | bytes 12582916 | tf_op jit(solution)/shard_map/while
  243.8 4.5 %copy-start.1 = (f32[8,128,1024]{2,1,0:T(8,128)S(1)}, f32[8,128,1024]{2,1,0:T(8,128)}, u32[]{:S(2)}) copy-start(f32[8,128,1024]{2,1,0:T(8,128)} %get-tuple-element.462) | copy-start | bytes 12582916 | tf_op jit(solution)/shard_map/while
  259.1 4.5 %copy-start.1 = (f32[8,128,1024]{2,1,0:T(8,128)S(1)}, f32[8,128,1024]{2,1,0:T(8,128)}, u32[]{:S(2)}) copy-start(f32[8,128,1024]{2,1,0:T(8,128)} %get-tuple-element.462) | copy-start | bytes 12582916 | tf_op jit(solution)/shard_map/while
  274.0 82.6 %reduce-scatter.5.cloned.1.call-start = ((), (), s32[]{:S(2)}) async-start(), calls=%async_computation.5 | async-start | bytes 2359296 | tf_op jit(solution)/shard_map/reduce_scatter | solution.py:143
  275.4 22.0 %collective-permute-start.7 = (bf16[1024,512]{1,0:T(8,128)(2,1)S(1)}, bf16[1024,512]{1,0:T(8,128)(2,1)S(1)}, u32[]{:S(2)}, u32[]{:S(2)}) collective-permute-start(bf16[1024,512]{1,0:T(8,128)(2,1)S(1)} %copy_bitcast_fusion.2), channel_id=1, source_target_pairs={{0,128},{8,136},{16,144},{24,152},{32,160},{40,168},{48,176},{56,1... | collective-permute-start | bytes 3145736 | tf_op jit(solution)/shard_map/ppermute | solution.py:15
  300.8 6.3 %copy-start.5 = (bf16[4,8,128,128]{3,2,1,0:T(8,128)(2,1)S(1)}, bf16[4,8,128,128]{3,2,1,0:T(8,128)(2,1)}, u32[]{:S(2)}) copy-start(bf16[4,8,128,128]{3,2,1,0:T(8,128)(2,1)} %get-tuple-element.116) | copy-start | bytes 3145732
  302.3 27.9 %collective-permute-start.5 = (bf16[128,4096]{1,0:T(8,128)(2,1)}, bf16[128,4096]{1,0:T(8,128)(2,1)}, u32[]{:S(2)}, u32[]{:S(2)}) collective-permute-start(bf16[128,4096]{1,0:T(8,128)(2,1)} %bitcast.228), channel_id=1, source_target_pairs={{0,128},{8,136},{16,144},{24,152},{32,160},{40,168},{48,176},{56,1... | collective-permute-start | bytes 3145736 | tf_op jit(solution)/shard_map/ppermute | solution.py:15
  304.1 41.9 %collective-permute-start.4 = (bf16[128,4096]{1,0:T(8,128)(2,1)}, bf16[128,4096]{1,0:T(8,128)(2,1)}, u32[]{:S(2)}, u32[]{:S(2)}) collective-permute-start(bf16[128,4096]{1,0:T(8,128)(2,1)} %copy.106), channel_id=1, source_target_pairs={{0,128},{8,136},{16,144},{24,152},{32,160},{40,168},{48,176},{56,1... | collective-permute-start | bytes 3145736 | tf_op jit(solution)/shard_map/ppermute | solution.py:15
  (22 other events, 44.2 us)
Sparse Core Ops, SparseCore 0:
  9.8 44.1 all-gather.4
  56.2 45.4 all-gather.2
  274.1 38.3 reduce-scatter.2
  315.5 41.0 reduce-scatter.4
where the time goes:
time: 365 us; the launch traced here: 363 us
  waiting for transfers between devices  153 us (42%)
  matrix products  97.6 us (27%)
  local copies, waits for them, and re-layouts  46.1 us (13%)
  other arithmetic  35.5 us (10%)
  starting transfers between devices  17 us (5%)
  between operations  13.9 us (4%)
    ppermute x8, waiting for transfers between devices, swapped(): lax.ppermute(x, axis, [(i, i ^ 1 << distance) for i in range(lax.axis_siz...  66.5 us
    all_gather x1, waiting for transfers between devices, body(): lax.all_gather(key_input, 'tensor', axis=0, tiled=True)  41.6 us
    sub x8, matrix products, one_group(): weights = jnp.exp(scores - row_max)  36 us
    all_gather x1, waiting for transfers between devices, body(): lax.all_gather(value_input, 'tensor', axis=0, tiled=True)  35.9 us
    convert_element_type x8, other arithmetic, one_group(): probs_low = attn_probs.astype(jnp.bfloat16)  22.9 us
    dot_general x8, matrix products, one_group(): jnp.einsum('gqk,kd->gqd', dscore, key_part, preferred_element_type=jnp.fl...  20.5 us
    ppermute x8, starting transfers between devices, swapped(): lax.ppermute(x, axis, [(i, i ^ 1 << distance) for i in range(lax.axis_siz...  16.9 us
    dot_general x8, matrix products, one_group(): jnp.einsum('gqk,kd->gqd', probs_low, value_part, preferred_element_type=j...  12.4 us
  transfers between devices with their start and end apart: 12, of which 7 were waited for; matrix products, arithmetic and copies ran while one was open for 28% of the time, Pallas kernels for 0%

commit v1 on v0

v1 whole, which is shorter than its diff:
```python
import math

import jax
import jax.numpy as jnp
from jax import lax
from jax.experimental import pallas as pl
from jax.experimental.pallas import tpu as pltpu
from jax.sharding import PartitionSpec as P

GROUPS = 8
REPEAT = 8
DEPTH = 128
ROWS = 128
RING = 8
PACK = ROWS * RING
WIDE = REPEAT * DEPTH
DOCS = 8
NEGATIVE = -1e30
SCALE = 1.0 / math.sqrt(DEPTH)
EXP2_SCALE = SCALE * math.log2(math.e)

UP = (4, 4, 4, 3, 3, 2, 1, 0)
DOWN = (3, 3, 3, 4, 0, 0, 0, 0)
HOPS = 4
TICKS = GROUPS + 2 * HOPS

MESH = pl.DeviceIdType.MESH
F32 = jnp.float32
BF16 = jnp.bfloat16


def product(a, b, left, right):
    return lax.dot_general(a, b, (((left,), (right,)), ((), ())), preferred_element_type=F32)


def kernel(
    query_hbm, key_hbm, value_hbm, grad_hbm, lengths,
    out_hbm, dquery_hbm, dkey_hbm, dvalue_hbm,
    query, grad, out, dquery, kv, terms, partial, second, bias, dkv,
    kv_in, up_out, down_out, part_in, second_in, part_out, load_sem, own_sem, store_sem, final_sem,
):
    dp = lax.axis_index("dp")
    z = lax.axis_index("tensor")
    above = lax.rem(z + 1, RING)
    below = lax.rem(z + RING - 1, RING)

    def columns(g, width):
        return pl.ds(pl.multiple_of(g * width, width), width)

    def own_copy(g, which):
        source = (key_hbm, value_hbm)[which]
        return pltpu.make_async_copy(
            source.at[:, columns(g, DEPTH)], kv.at[g, z, which], own_sem.at[g, which]
        )

    load_query = pltpu.make_async_copy(query_hbm, query, load_sem.at[0])
    load_grad = pltpu.make_async_copy(grad_hbm, grad, load_sem.at[1])

    for g in range(GROUPS):
        own_copy(g, 0).start()
        own_copy(g, 1).start()
    load_query.start()
    load_grad.start()

    barrier = pltpu.get_barrier_semaphore()
    for neighbour in (above, below):
        pl.semaphore_signal(barrier, inc=1, device_id=(dp, neighbour), device_id_type=MESH)

    for b in range(HOPS, RING):
        @pl.when(z < b)
        def _(b=b):
            for g in range(GROUPS):
                kv[g, b] = jnp.zeros((2, ROWS, DEPTH), BF16)

    row_pos = z * ROWS + lax.broadcasted_iota(jnp.int32, (ROWS, PACK), 0)
    col_pos = lax.broadcasted_iota(jnp.int32, (ROWS, PACK), 1)
    row_doc = jnp.zeros((ROWS, PACK), jnp.int32)
    col_doc = jnp.zeros((ROWS, PACK), jnp.int32)
    end = jnp.int32(0)
    for k in range(DOCS):
        end = end + lengths[dp, k]
        row_doc = row_doc + (row_pos >= end).astype(jnp.int32)
        col_doc = col_doc + (col_pos >= end).astype(jnp.int32)
    bias[...] = jnp.where((row_doc == col_doc) & (col_pos <= row_pos), 0.0, NEGATIVE)

    pl.semaphore_wait(barrier, 2)

    def send_up(g, b):
        return pltpu.make_async_remote_copy(
            src_ref=kv.at[g, b], dst_ref=kv.at[g, b], send_sem=up_out.at[g, b],
            recv_sem=kv_in.at[g, b], device_id=(dp, above), device_id_type=MESH,
        )

    def send_down(g, b):
        return pltpu.make_async_remote_copy(
            src_ref=kv.at[g, b], dst_ref=kv.at[g, b], send_sem=down_out.at[g, b],
            recv_sem=kv_in.at[g, b], device_id=(dp, below), device_id_type=MESH,
        )

    def from_below(hop):
        return z - hop, (z >= hop) & ((z < RING - 1) | (hop < 4))

    def goes_up(hop):
        return (z >= hop) & (z < RING - 1) & (hop < 4) & ((z < RING - 2) | (hop < 3))

    def from_above(hop):
        b = lax.rem(z + hop, RING)
        return b, (b <= 3) & ((b == 3) | (hop <= 3))

    def goes_down(hop):
        b = lax.rem(z + hop, RING)
        return (b <= 3) & (hop < 4) & ((b == 3) | (hop < 3))

    def gather_step(g, hop):
        b, comes = from_below(hop)

        @pl.when(comes)
        def _():
            send_up(g, b).wait_recv()

        @pl.when(goes_up(hop))
        def _():
            send_up(g, b).start()

        c, falls = from_above(hop)

        @pl.when(falls)
        def _():
            send_down(g, c).wait_recv()

        @pl.when(goes_down(hop))
        def _():
            send_down(g, c).start()

    def gather_sent(g):
        for hop in range(HOPS):
            @pl.when(goes_up(hop))
            def _(hop=hop):
                send_up(g, z - hop).wait_send()

            @pl.when(goes_down(hop))
            def _(hop=hop):
                send_down(g, lax.rem(z + hop, RING)).wait_send()

    def pass_down(source, g, b):
        return pltpu.make_async_remote_copy(
            src_ref=source.at[g, b], dst_ref=partial.at[g, b], send_sem=part_out.at[g, b],
            recv_sem=part_in.at[g, b], device_id=(dp, below), device_id_type=MESH,
        )

    def pass_up(source, g, b, last):
        return pltpu.make_async_remote_copy(
            src_ref=source.at[g, b],
            dst_ref=second.at[g] if last else partial.at[g, b],
            send_sem=part_out.at[g, b],
            recv_sem=second_in.at[g] if last else part_in.at[g, b],
            device_id=(dp, above), device_id_type=MESH,
        )

    def add_own(g, b):
        total = partial[g, b].astype(F32) + terms[g, b].astype(F32)
        partial[g, b] = total.astype(BF16)

    def return_step(g, phase):
        for b in range(RING):
            distance = UP[b] - phase
            if UP[b] and distance > 0:
                @pl.when(z == b + distance)
                def _(b=b):
                    if phase:
                        pass_down(partial, g, b).wait_recv()
                        add_own(g, b)
                        pass_down(partial, g, b).start()
                    else:
                        pass_down(terms, g, b).start()
            distance = DOWN[b] - phase
            if DOWN[b] and distance > 0:
                place = (b - distance) % RING

                @pl.when(z == place)
                def _(b=b, distance=distance, place=place):
                    if phase:
                        pass_up(partial, g, b, False).wait_recv()
                        if place > b:
                            add_own(g, b)
                        pass_up(partial, g, b, distance == 1).start()
                    else:
                        pass_up(terms, g, b, distance == 1).start()

    def return_end(g):
        dkv[...] = terms[g, z].astype(F32)

        @pl.when(z < RING - 1)
        def _():
            pass_down(partial, g, z).wait_recv()
            dkv[...] += partial[g, z].astype(F32)

        @pl.when(z < 4)
        def _():
            pass_up(partial, g, z, True).wait_recv()
            dkv[...] += second[g].astype(F32)

        terms[g, z] = dkv[...].astype(BF16)
        final_copy(g, 0).start()
        final_copy(g, 1).start()

    def final_copy(g, which):
        target = (dkey_hbm, dvalue_hbm)[which]
        return pltpu.make_async_copy(
            terms.at[g, z, which], target.at[:, columns(g, DEPTH)], final_sem.at[g, which]
        )

    def return_sent(g):
        for b in range(RING):
            if UP[b]:
                @pl.when((z > b) & (z <= b + UP[b]))
                def _(b=b):
                    pass_down(partial, g, b).wait_send()
            if DOWN[b]:
                away = lax.rem(b - z + RING, RING)

                @pl.when((away > 0) & (away <= DOWN[b]))
                def _(b=b):
                    pass_up(partial, g, b, False).wait_send()

    def store_copy(g, which):
        source, target = ((out, out_hbm), (dquery, dquery_hbm))[which]
        return pltpu.make_async_copy(
            source.at[:, columns(g, WIDE)], target.at[:, columns(g, WIDE)], store_sem.at[g, which]
        )

    def attend(g):
        keys = kv[g, :, 0].reshape(PACK, DEPTH)
        values = kv[g, :, 1].reshape(PACK, DEPTH)
        heads = [columns(g * REPEAT + h, DEPTH) for h in range(REPEAT)]
        queries = jnp.concatenate([query[:, c] for c in heads], axis=0)
        grads = jnp.concatenate([grad[:, c] for c in heads], axis=0)
        scores = product(queries, keys, 1, 1) + jnp.concatenate([bias[...]] * REPEAT, axis=0)
        row_max = jnp.max(scores, axis=1, keepdims=True)
        weights = jnp.exp2((scores - row_max) * EXP2_SCALE).astype(BF16)
        values_ones = jnp.concatenate([values, jnp.ones((PACK, DEPTH), BF16)], axis=1)
        summed = product(weights, values_ones, 1, 0)
        inverse = 1.0 / summed[:, DEPTH:]
        attn_out = (summed[:, :DEPTH] * inverse).astype(BF16)
        grads = (grads.astype(F32) * inverse).astype(BF16)
        delta = jnp.sum(grads.astype(F32) * attn_out.astype(F32), axis=1, keepdims=True)
        dprobs = product(grads, values, 1, 1)
        dscore = (dprobs - delta).astype(BF16) * weights
        dqueries = (product(dscore, keys, 1, 0) * SCALE).astype(BF16)
        for h, c in enumerate(heads):
            out[:, c] = attn_out[h * ROWS:(h + 1) * ROWS]
            dquery[:, c] = dqueries[h * ROWS:(h + 1) * ROWS]
        store_copy(g, 0).start()
        store_copy(g, 1).start()
        key_terms = (product(dscore, queries, 0, 0) * SCALE).astype(BF16)
        value_terms = product(weights, grads, 0, 0).astype(BF16)
        terms[g, :, 0] = key_terms.reshape(RING, ROWS, DEPTH)
        terms[g, :, 1] = value_terms.reshape(RING, ROWS, DEPTH)

    def in_range(g):
        return (g >= 0) & (g < GROUPS)

    def tick(t, _):
        for hop in range(HOPS, -1, -1):
            @pl.when(in_range(t - hop))
            def _(hop=hop):
                if hop == 0:
                    own_copy(t, 0).wait()
                    own_copy(t, 1).wait()
                gather_step_any(t - hop, hop)

        g = t - HOPS

        @pl.when(t == HOPS)
        def _():
            load_query.wait()
            load_grad.wait()

        @pl.when(in_range(g))
        def _():
            attend(g)

        for phase in range(HOPS, -1, -1):
            @pl.when(in_range(g - phase))
            def _(phase=phase):
                if phase == HOPS:
                    return_end(g - phase)
                else:
                    return_step(g - phase, phase)

        return 0

    def gather_step_any(g, hop):
        if hop:
            gather_step(g, hop)
        else:
            @pl.when(goes_up(0))
            def _():
                send_up(g, z).start()

            @pl.when(goes_down(0))
            def _():
                send_down(g, z).start()

    lax.fori_loop(0, TICKS, tick, 0)

    def finish(g, _):
        gather_sent(g)
        return_sent(g)
        for which in range(2):
            store_copy(g, which).wait()
            final_copy(g, which).wait()
        return 0

    lax.fori_loop(0, GROUPS, finish, 0)


def body(query_input, key_input, value_input, output_gradient, document_lengths):
    anywhere = pl.BlockSpec(memory_space=pl.ANY)
    wide = jax.ShapeDtypeStruct((ROWS, GROUPS * WIDE), BF16)
    narrow = jax.ShapeDtypeStruct((ROWS, GROUPS * DEPTH), BF16)
    rows = pltpu.VMEM((ROWS, GROUPS * WIDE), BF16)
    blocks = pltpu.VMEM((GROUPS, RING, 2, ROWS, DEPTH), BF16)
    sems = pltpu.SemaphoreType.DMA
    return pl.pallas_call(
        kernel,
        out_shape=(wide, wide, narrow, narrow),
        in_specs=[anywhere] * 4 + [pl.BlockSpec(memory_space=pltpu.SMEM)],
        out_specs=(anywhere,) * 4,
        scratch_shapes=[
            rows, rows, rows, rows,
            blocks, blocks, blocks,
            pltpu.VMEM((GROUPS, 2, ROWS, DEPTH), BF16),
            pltpu.VMEM((ROWS, PACK), F32),
            pltpu.VMEM((2, ROWS, DEPTH), F32),
            sems((GROUPS, RING)), sems((GROUPS, RING)), sems((GROUPS, RING)),
            sems((GROUPS, RING)), sems((GROUPS,)), sems((GROUPS, RING)),
            sems((2,)), sems((GROUPS, 2)), sems((GROUPS, 2)), sems((GROUPS, 2)),
        ],
        compiler_params=pltpu.CompilerParams(
            collective_id=0, has_side_effects=True, vmem_limit_bytes=56 * 2**20
        ),
    )(query_input, key_input, value_input, output_gradient, document_lengths)


def solution(mesh):
    rows = P(("dp", "tensor"), None)
    return jax.shard_map(
        body,
        mesh=mesh,
        in_specs=(rows, rows, rows, rows, P()),
        out_specs=(rows, rows, rows, rows),
        check_vma=False,
    )
```

time: 365 us -> 110 us (0.30)
  waiting for transfers between devices: 153 us -> 0 us
  Pallas kernels: 0 us -> 102 us
  matrix products: 97.6 us -> 0 us
  local copies, waits for them, and re-layouts: 46.1 us -> 7.35 us
  other arithmetic: 35.5 us -> 0 us
  starting transfers between devices: 17 us -> 0 us
  between operations: 13.9 us -> 0.65 us
    pallas_call x0 -> x1, Pallas kernels: none -> 102 us  [body(): pl.pallas_call(kernel, out_shape=(wide, wide, narrow, narrow), in_specs=[...]
    all_gather x2 -> x0, waiting for transfers between devices: 77.5 us -> none  [the longest x1 41.6 us: body(): lax.all_gather(key_input, 'tensor', axis=0, tiled=True)]
    ppermute x8 -> x0, waiting for transfers between devices: 66.5 us -> none  [swapped(): lax.ppermute(x, axis, [(i, i ^ 1 << distance) for i in range(lax.axis_siz...]
    dot_general x40 -> x0, matrix products: 61.6 us -> none  [the longest x8 20.5 us: one_group(): jnp.einsum('gqk,kd->gqd', dscore, key_part, preferred_element_type=jnp.fl...]
    sub x8 -> x0, matrix products: 36 us -> none  [one_group(): weights = jnp.exp(scores - row_max)]
    convert_element_type x8 -> x0, other arithmetic: 22.9 us -> none  [one_group(): probs_low = attn_probs.astype(jnp.bfloat16)]
    ppermute x8 -> x0, starting transfers between devices: 16.9 us -> none  [swapped(): lax.ppermute(x, axis, [(i, i ^ 1 << distance) for i in range(lax.axis_siz...]
    slice x6 -> x0, local copies, waits for them, and re-layouts: 11.6 us -> none  [the longest x2 4.56 us: body(): values_all[:, :key_split]]
  transfers between devices with their start and end apart: 12 -> 0, of which waited for: 7 -> 0; matrix products, arithmetic and copies ran while one was open for 28% -> 0% of each run, Pallas kernels for 0% -> 0%
where the time goes in v1:
time: 110 us
  Pallas kernels  102 us (93%)
  local copies, waits for them, and re-layouts  7.35 us (7%)
    pallas_call x1, Pallas kernels, body(): pl.pallas_call(kernel, out_shape=(wide, wide, narrow, narrow), in_specs=[...  102 us
    unnamed x11, local copies, waits for them, and re-layouts  7.35 us

profile of v1, /device:TPU:6, one launch (start us, length us, event | category | flops | bytes accessed | tf_op | source)
XLA Modules:
  0.0 109.6 jit_solution(5152253791756401191)
XLA Ops:
  0.6 1.4 %copy.9.lengths = s32[32,8]{1,0:T(8,128)} copy(s32[32,8]{0,1:T(8,128)} %param.9) | data formatting | bytes 2048 | tf_op args[4]
  2.0 101.6 %shard_map.84 = (bf16[128,8192]{1,0:T(8,128)(2,1)}, bf16[128,8192]{1,0:T(8,128)(2,1)}, bf16[128,1024]{1,0:T(8,128)(2,1)}, bf16[128,1024]{1,0:T(8,128)(2,1)}) custom-call(bf16[128,8192]{1,0:T(8,128)(2,1)} %query_hbm.1, bf16[128,1024]{1,0:T(8,128)(2,1)} %key_hbm.1, bf16[128,1024]{1,0:T(8,128)(2,1)} %value_hbm.1, bf16[128,8192]{1,0:T(8,128)(2,1)} %grad_hbm.1, ...), custom_call_target="tpu_custom_call" | custom-call | tf_op jit(solution)/shard_map/pallas_call | solution.py:325
  103.7 0.0 copy-start
  103.7 3.2 %copy.14 = bf16[128,8192]{1,0:T(8,128)(2,1)} copy(bf16[128,8192]{1,0:T(8,128)(2,1)} %get-tuple-element.8) | data formatting | bytes 4194304
  106.9 0.0 copy-done
  106.9 0.0 copy-start.2
  106.9 0.0 copy-start.1
  106.9 1.3 %copy.15 = bf16[128,8192]{1,0:T(8,128)(2,1)} copy(bf16[128,8192]{1,0:T(8,128)(2,1)S(1)} %copy-done) | data formatting | bytes 4194304
  108.2 0.0 copy-done.2
  108.2 0.7 copy.16
  108.9 0.0 copy-done.1
  108.9 0.7 copy.17
Async XLA Ops:
  103.7 3.3 %copy-start = (bf16[128,8192]{1,0:T(8,128)(2,1)S(1)}, bf16[128,8192]{1,0:T(8,128)(2,1)}, u32[]{:S(2)}) copy-start(bf16[128,8192]{1,0:T(8,128)(2,1)} %get-tuple-element.9) | copy-start | bytes 6291460
  106.9 1.3 %copy-start.2 = (bf16[128,1024]{1,0:T(8,128)(2,1)S(1)}, bf16[128,1024]{1,0:T(8,128)(2,1)}, u32[]{:S(2)}) copy-start(bf16[128,1024]{1,0:T(8,128)(2,1)} %get-tuple-element.10) | copy-start | bytes 786436
  106.9 2.0 %copy-start.1 = (bf16[128,1024]{1,0:T(8,128)(2,1)S(1)}, bf16[128,1024]{1,0:T(8,128)(2,1)}, u32[]{:S(2)}) copy-start(bf16[128,1024]{1,0:T(8,128)(2,1)} %get-tuple-element.11) | copy-start | bytes 786436

commit v2 on v1

v2 whole, which is shorter than its diff:
```python
import math

import jax
import jax.numpy as jnp
from jax import lax
from jax.experimental import pallas as pl
from jax.experimental.pallas import tpu as pltpu
from jax.sharding import PartitionSpec as P

GROUPS = 8
REPEAT = 8
DEPTH = 128
ROWS = 128
RING = 8
PACK = ROWS * RING
WIDE = REPEAT * DEPTH
DOCS = 8
PACKS = 32
NEGATIVE = -1e30
SCALE = 1.0 / math.sqrt(DEPTH)
EXP2_SCALE = SCALE * math.log2(math.e)

STREAMS = 1
UP = ((4, 4, 4, 3, 3, 2, 1, 0),)
DOWN = ((3, 3, 3, 4, 0, 0, 0, 0),)

OWN_UP, OWN_DOWN, FROM_BELOW, FROM_ABOVE, END_UP, END_DOWN, BACK_DOWN, BACK_UP, FINAL = range(9)
PARTS = 1
FIRST_TICK = -7
LAST_TICK = GROUPS - 1 + 7
PLAN = (
    (
        ((7, 1, 5), (3, 2, -1), (8, 0, 7), (7, 2, 3), (3, 1, -2), (3, 3, -1), (7, 3, 2), (1, 0, -7),
         (0, 0, -7),),
    ),
    (
        ((7, 2, 4), (3, 2, -4), (7, 3, 2), (3, 3, -4), (6, 0, 4), (1, 1, -6), (8, 1, 5), (0, 1, -7),
         (2, 0, -5),),
    ),
    (
        ((6, 0, 2), (6, 1, 3), (0, 2, -5), (2, 0, -3), (1, 2, -5), (7, 3, 3), (2, 1, -5), (8, 2, 5),
         (3, 3, -5),),
    ),
    (
        ((1, 3, -6), (2, 0, -2), (8, 3, 7), (0, 3, -6), (6, 0, 1), (6, 1, 2), (6, 2, 3), (2, 2, -4),
         (2, 1, -4),),
    ),
    (
        ((2, 2, -2), (4, 0, 0), (2, 1, -2), (6, 2, 2), (0, 4, -6), (8, 4, 5), (2, 3, -4), (6, 3, 3),
         (6, 1, 0), (2, 0, -1),),
    ),
    (
        ((4, 1, 0), (2, 2, -1), (6, 3, 2), (2, 4, -3), (5, 0, 1), (2, 3, -2), (0, 5, -7), (6, 2, 1),
         (6, 4, 3), (8, 5, 7), (3, 0, -2), (2, 1, -1),),
    ),
    (
        ((4, 2, 0), (4, 3, 0), (2, 4, -2), (0, 6, -6), (7, 0, 2), (3, 0, -5), (3, 1, -1), (6, 4, 1),
         (2, 3, -1), (8, 6, 5), (5, 1, 0), (6, 5, 3), (2, 5, -3), (2, 2, -1),),
    ),
    (
        ((4, 4, 0), (5, 3, 0), (3, 1, -2), (3, 0, -6), (2, 6, -2), (7, 0, 3), (5, 2, 0), (4, 5, 0),
         (4, 6, 1), (2, 5, -1), (3, 2, -1), (2, 4, -1), (3, 3, -1), (7, 1, 1), (8, 7, 0),),
    ),
)

MESH = pl.DeviceIdType.MESH
F32 = jnp.float32
BF16 = jnp.bfloat16


def product(a, b, left, right):
    return lax.dot_general(a, b, (((left,), (right,)), ((), ())), preferred_element_type=F32)


def kernel(
    query_hbm, key_hbm, value_hbm, grad_hbm, lengths_hbm,
    out, dquery, dkv_out,
    lengths, query, grad, kv, terms, partial, second, bias, dkv,
    kv_in, up_out, down_out, part_in, second_in, part_out, load_sem, own_sem,
):
    dp = lax.axis_index("dp")
    z = lax.axis_index("tensor")
    above = lax.rem(z + 1, RING)
    below = lax.rem(z + RING - 1, RING)

    def columns(g, width):
        return pl.ds(pl.multiple_of(g * width, width), width)

    def own_copy(g, which):
        source = (key_hbm, value_hbm)[which]
        return pltpu.make_async_copy(
            source.at[:, columns(g, DEPTH)], kv.at[g, z, which], own_sem.at[g, which]
        )

    load_query = pltpu.make_async_copy(query_hbm, query, load_sem.at[0])
    load_grad = pltpu.make_async_copy(grad_hbm, grad, load_sem.at[1])
    load_lengths = pltpu.make_async_copy(lengths_hbm, lengths, load_sem.at[2])

    barrier = pltpu.get_barrier_semaphore()
    for neighbour in (above, below):
        pl.semaphore_signal(barrier, inc=1, device_id=(dp, neighbour), device_id_type=MESH)

    load_lengths.start()
    for g in range(GROUPS):
        own_copy(g, 0).start()
        own_copy(g, 1).start()
    load_query.start()
    load_grad.start()

    def piece(s):
        return (s,) if STREAMS > 1 else ()

    for s in range(STREAMS):
        for b in range(1, RING):
            if not DOWN[s][b]:
                @pl.when(z < b)
                def _(b=b, s=s):
                    for g in range(GROUPS):
                        at = (g, b) + piece(s)
                        kv[at] = jnp.zeros(kv.at[at].shape, BF16)

    load_lengths.wait()
    row_pos = z * ROWS + lax.broadcasted_iota(jnp.int32, (PACK, ROWS), 1)
    col_pos = lax.broadcasted_iota(jnp.int32, (PACK, ROWS), 0)
    row_doc = jnp.zeros((PACK, ROWS), jnp.int32)
    col_doc = jnp.zeros((PACK, ROWS), jnp.int32)
    end = jnp.int32(0)
    for k in range(DOCS):
        end = end + lengths[k, dp]
        row_doc = row_doc + (row_pos >= end).astype(jnp.int32)
        col_doc = col_doc + (col_pos >= end).astype(jnp.int32)
    bias[...] = jnp.where((row_doc == col_doc) & (col_pos <= row_pos), 0.0, NEGATIVE)

    def forward(g, b, s, up):
        here = kv.at[(g, b) + piece(s)]
        return pltpu.make_async_remote_copy(
            src_ref=here, dst_ref=here, send_sem=(up_out if up else down_out).at[g, b, s],
            recv_sem=kv_in.at[g, b, s], device_id=(dp, above if up else below), device_id_type=MESH,
        )

    def back(source, g, b, s, up, last=False):
        at = (g, b) + piece(s)
        return pltpu.make_async_remote_copy(
            src_ref=source.at[at],
            dst_ref=second.at[(g,) + piece(s)] if last else partial.at[at],
            send_sem=part_out.at[g, b, s],
            recv_sem=second_in.at[g, s] if last else part_in.at[g, b, s],
            device_id=(dp, above if up else below), device_id_type=MESH,
        )

    def add_own(g, b, s):
        at = (g, b) + piece(s)
        partial[at] = (partial[at].astype(F32) + terms[at].astype(F32)).astype(BF16)

    def step(kind, place, b, s, g):
        if kind == OWN_UP:
            forward(g, b, s, True).start()
        elif kind == OWN_DOWN:
            forward(g, b, s, False).start()
        elif kind == FROM_BELOW:
            forward(g, b, s, True).wait_recv()
            if place - b < UP[s][b]:
                forward(g, b, s, True).start()
        elif kind == FROM_ABOVE:
            forward(g, b, s, False).wait_recv()
            if (b - place) % RING < DOWN[s][b]:
                forward(g, b, s, False).start()
        elif kind == END_UP:
            back(terms, g, b, s, False).start()
        elif kind == END_DOWN:
            back(terms, g, b, s, True, (b - place) % RING == 1).start()
        elif kind == BACK_DOWN:
            back(partial, g, b, s, False).wait_recv()
            add_own(g, b, s)
            back(partial, g, b, s, False).start()
        elif kind == BACK_UP:
            back(partial, g, b, s, True).wait_recv()
            if place > b:
                add_own(g, b, s)
            back(partial, g, b, s, True, (b - place) % RING == 1).start()
        else:
            at = (g, b) + piece(s)
            total = terms[at].astype(F32)
            if UP[s][b]:
                back(partial, g, b, s, False).wait_recv()
                total = total + partial[at].astype(F32)
            if DOWN[s][b]:
                back(partial, g, b, s, True, True).wait_recv()
                total = total + second[(g,) + piece(s)].astype(F32)
            dkv_out[(g,) + piece(s)] = total.astype(BF16)

    def sent(g):
        for place in range(RING):
            @pl.when(z == place)
            def _(place=place):
                for entry in [entry for part in PLAN[place] for entry in part]:
                    kind, b = entry[:2]
                    s = entry[3] if STREAMS > 1 else 0
                    if kind == OWN_UP or (kind == FROM_BELOW and place - b < UP[s][b]):
                        forward(g, b, s, True).wait_send()
                    elif kind == OWN_DOWN or (
                        kind == FROM_ABOVE and (b - place) % RING < DOWN[s][b]
                    ):
                        forward(g, b, s, False).wait_send()
                    elif kind in (END_UP, BACK_DOWN, END_DOWN, BACK_UP):
                        back(partial, g, b, s, kind in (END_DOWN, BACK_UP)).wait_send()

    def attend(g, part):
        keys = kv[g, :, 0].reshape(PACK, DEPTH)
        values = kv[g, :, 1].reshape(PACK, DEPTH)
        count = REPEAT // PARTS
        heads = [columns(g * REPEAT + part * count + h, DEPTH) for h in range(count)]
        queries = jnp.concatenate([query[:, c] for c in heads], axis=0)
        grads = jnp.concatenate([grad[:, c] for c in heads], axis=0)
        scores = product(keys, queries, 1, 1) + jnp.concatenate([bias[...]] * count, axis=1)
        row_max = jnp.max(scores, axis=0, keepdims=True)
        raised = jnp.exp2((scores - row_max) * EXP2_SCALE)
        inverse = 1.0 / jnp.sum(raised, axis=0, keepdims=True)
        weights = raised.astype(BF16)
        attn_out = (product(values, weights, 0, 0) * inverse).T.astype(BF16)
        grads = (grads.astype(F32) * jnp.broadcast_to(inverse, (DEPTH, count * ROWS)).T).astype(BF16)
        delta = jnp.sum(grads.astype(F32) * attn_out.astype(F32), axis=1, keepdims=True)
        delta = jnp.broadcast_to(delta, (count * ROWS, DEPTH)).T[:1]
        dscore = (product(values, grads, 1, 1) - delta).astype(BF16) * weights
        dqueries = (product(keys, dscore, 0, 0).T * SCALE).astype(BF16)
        for h, c in enumerate(heads):
            out[:, c] = attn_out[h * ROWS:(h + 1) * ROWS]
            dquery[:, c] = dqueries[h * ROWS:(h + 1) * ROWS]
        key_terms = product(dscore, queries, 1, 0)
        value_terms = product(weights, grads, 1, 0)
        if part:
            key_terms = key_terms + dkv[0]
            value_terms = value_terms + dkv[1]
        if part < PARTS - 1:
            dkv[0] = key_terms
            dkv[1] = value_terms
        else:
            terms[g, :, 0] = (key_terms * SCALE).astype(BF16).reshape(RING, ROWS, DEPTH)
            terms[g, :, 1] = value_terms.astype(BF16).reshape(RING, ROWS, DEPTH)

    def in_range(g):
        return (g >= 0) & (g < GROUPS)

    def tick(index, _):
        t = index + FIRST_TICK

        @pl.when(t == 0)
        def _():
            load_query.wait()
            load_grad.wait()

        for part in range(PARTS):
            @pl.when(in_range(t))
            def _(part=part):
                attend(t, part)

            for place in range(RING):
                @pl.when(z == place)
                def _(part=part, place=place):
                    for entry in PLAN[place][part]:
                        kind, b, offset = entry[:3]

                        @pl.when(in_range(t - offset))
                        def _(entry=entry, kind=kind, b=b, offset=offset):
                            step(kind, place, b, entry[3] if STREAMS > 1 else 0, t - offset)

        return 0

    for g in range(GROUPS):
        own_copy(g, 0).wait()
        own_copy(g, 1).wait()
    pl.semaphore_wait(barrier, 2)

    lax.fori_loop(0, LAST_TICK + 1 - FIRST_TICK, tick, 0)

    def finish(g, _):
        sent(g)
        return 0

    lax.fori_loop(0, GROUPS, finish, 0)


def store(out, dquery, dkv, out_hbm, dquery_hbm, dkey_hbm, dvalue_hbm, sem):
    copies = [
        pltpu.make_async_copy(out, out_hbm, sem.at[0]),
        pltpu.make_async_copy(dquery, dquery_hbm, sem.at[1]),
    ]
    for g in range(GROUPS):
        place = pl.ds(g * DEPTH, DEPTH)
        for which, target in enumerate((dkey_hbm, dvalue_hbm)):
            copies.append(pltpu.make_async_copy(
                dkv.at[g, which], target.at[:, place], sem.at[2 + 2 * g + which]
            ))
    for copy in copies:
        copy.start()
    for copy in copies:
        copy.wait()


def body(query_input, key_input, value_input, output_gradient, document_lengths):
    hbm = pl.BlockSpec(memory_space=pltpu.HBM)
    wide = jax.ShapeDtypeStruct((ROWS, GROUPS * WIDE), BF16)
    narrow = jax.ShapeDtypeStruct((ROWS, GROUPS * DEPTH), BF16)
    rows = pltpu.VMEM((ROWS, GROUPS * WIDE), BF16)
    blocks = pltpu.VMEM((GROUPS, RING, 2, ROWS, DEPTH), BF16)
    gathered = pltpu.VMEM((GROUPS, 2, ROWS, DEPTH), BF16)
    sems = pltpu.SemaphoreType.DMA
    each = sems((GROUPS, RING, STREAMS))
    inputs = [
        pltpu.with_memory_space_constraint(x, pltpu.HBM)
        for x in (query_input, key_input, value_input, output_gradient, document_lengths.T)
    ]
    held = pl.pallas_call(
        kernel,
        out_shape=(rows, rows, gathered),
        in_specs=[hbm] * 5,
        out_specs=(pl.BlockSpec(memory_space=pltpu.VMEM),) * 3,
        scratch_shapes=[
            pltpu.SMEM((DOCS, PACKS), jnp.int32),
            rows, rows,
            blocks, blocks, blocks, gathered,
            pltpu.VMEM((PACK, ROWS), F32),
            pltpu.VMEM((2, PACK, DEPTH), F32),
            each, each, each, each, sems((GROUPS, STREAMS)), each,
            sems((3,)), sems((GROUPS, 2)),
        ],
        compiler_params=pltpu.CompilerParams(
            collective_id=0, has_side_effects=True, vmem_limit_bytes=48 * 2**20
        ),
    )(*inputs)
    return pl.pallas_call(
        store,
        out_shape=(wide, wide, narrow, narrow),
        in_specs=[pl.BlockSpec(memory_space=pl.ANY)] * 3,
        out_specs=(hbm,) * 4,
        scratch_shapes=[sems((2 + 2 * GROUPS,))],
        compiler_params=pltpu.CompilerParams(vmem_limit_bytes=2**20),
    )(*held)


def solution(mesh):
    rows = P(("dp", "tensor"), None)
    return jax.shard_map(
        body,
        mesh=mesh,
        in_specs=(rows, rows, rows, rows, P()),
        out_specs=(rows, rows, rows, rows),
        check_vma=False,
    )
```

time: 110 us -> 87.6 us (0.80)
  Pallas kernels: 102 us -> 86.8 us
  local copies, waits for them, and re-layouts: 7.35 us -> 0 us
    pallas_call x1 -> x2, Pallas kernels: 102 us -> 86.8 us  [the longest x1 84.5 us: body(): pl.pallas_call(kernel, out_shape=(rows, rows, gathered), in_specs=[hbm] *...]
    unnamed x11 -> x0, local copies, waits for them, and re-layouts: 7.35 us -> none
where the time goes in v2:
time: 87.6 us; the launch traced here: 87.5 us
  Pallas kernels  86.8 us (99%)
    pallas_call x1, Pallas kernels, body(): pl.pallas_call(kernel, out_shape=(rows, rows, gathered), in_specs=[hbm] *...  84.5 us
    pallas_call x1, Pallas kernels, body(): pl.pallas_call(store, out_shape=(wide, wide, narrow, narrow), in_specs=[p...  2.3 us

profile of v2, /device:TPU:6, one launch (start us, length us, event | category | flops | bytes accessed | tf_op | source)
XLA Modules:
  0.0 87.5 jit_solution(10476084479766914020)
XLA Ops:
  0.6 84.5 %shard_map.84 = (bf16[128,8192]{1,0:T(8,128)(2,1)S(1)}, bf16[128,8192]{1,0:T(8,128)(2,1)S(1)}, bf16[8,2,128,128]{3,2,1,0:T(8,128)(2,1)S(1)}) custom-call(bf16[128,8192]{1,0:T(8,128)(2,1)} %query_hbm.1, bf16[128,1024]{1,0:T(8,128)(2,1)} %key_hbm.1, bf16[128,1024]{1,0:T(8,128)(2,1)} %value_hbm.1, bf16[128,8192]{1,0:T(8,128)(2,1)} %grad_hbm.1, s32[8,32]{1,0:T(8,128)} %bitcast.1), custom_call_target="tpu_custom_call" | custom-call | tf_op jit(solution)/shard_map/pallas_call | solution.py:313
  85.2 2.3 %shard_map.85 = (bf16[128,8192]{1,0:T(8,128)(2,1)}, bf16[128,8192]{1,0:T(8,128)(2,1)}, bf16[128,1024]{1,0:T(8,128)(2,1)}, bf16[128,1024]{1,0:T(8,128)(2,1)}) custom-call(bf16[128,8192]{1,0:T(8,128)(2,1)S(1)} %get-tuple-element.7.out, bf16[128,8192]{1,0:T(8,128)(2,1)S(1)} %get-tuple-element.8.dquery, bf16[8,2,128,128]{3,2,1,0:T(8,128)(2,1)S(1)} %get-tuple-element.9.dkv), custom_call_target="tpu_custom_call" | custom-call | tf_op jit(solution)/shard_map/pallas_call | solution.py:331

commit v3 on v2

--- a/solution.py
+++ b/solution.py
@@ -110,27 +110,6 @@
     def piece(s):
         return (s,) if STREAMS > 1 else ()
 
-    for s in range(STREAMS):
-        for b in range(1, RING):
-            if not DOWN[s][b]:
-                @pl.when(z < b)
-                def _(b=b, s=s):
-                    for g in range(GROUPS):
-                        at = (g, b) + piece(s)
-                        kv[at] = jnp.zeros(kv.at[at].shape, BF16)
-
-    load_lengths.wait()
-    row_pos = z * ROWS + lax.broadcasted_iota(jnp.int32, (PACK, ROWS), 1)
-    col_pos = lax.broadcasted_iota(jnp.int32, (PACK, ROWS), 0)
-    row_doc = jnp.zeros((PACK, ROWS), jnp.int32)
-    col_doc = jnp.zeros((PACK, ROWS), jnp.int32)
-    end = jnp.int32(0)
-    for k in range(DOCS):
-        end = end + lengths[k, dp]
-        row_doc = row_doc + (row_pos >= end).astype(jnp.int32)
-        col_doc = col_doc + (col_pos >= end).astype(jnp.int32)
-    bias[...] = jnp.where((row_doc == col_doc) & (col_pos <= row_pos), 0.0, NEGATIVE)
-
     def forward(g, b, s, up):
         here = kv.at[(g, b) + piece(s)]
         return pltpu.make_async_remote_copy(
@@ -150,7 +129,7 @@
 
     def add_own(g, b, s):
         at = (g, b) + piece(s)
-        partial[at] = (partial[at].astype(F32) + terms[at].astype(F32)).astype(BF16)
+        partial[at] = partial[at] + terms[at]
 
     def step(kind, place, b, s, g):
         if kind == OWN_UP:
@@ -238,11 +217,37 @@
             terms[g, :, 0] = (key_terms * SCALE).astype(BF16).reshape(RING, ROWS, DEPTH)
             terms[g, :, 1] = value_terms.astype(BF16).reshape(RING, ROWS, DEPTH)
 
+    def prepare():
+        for s in range(STREAMS):
+            for b in range(1, RING):
+                if not DOWN[s][b]:
+                    @pl.when(z < b)
+                    def _(b=b, s=s):
+                        for g in range(GROUPS):
+                            at = (g, b) + piece(s)
+                            kv[at] = jnp.zeros(kv.at[at].shape, BF16)
+
+        load_lengths.wait()
+        row_pos = z * ROWS + lax.broadcasted_iota(jnp.int32, (PACK, ROWS), 1)
+        col_pos = lax.broadcasted_iota(jnp.int32, (PACK, ROWS), 0)
+        row_doc = jnp.zeros((PACK, ROWS), jnp.int32)
+        col_doc = jnp.zeros((PACK, ROWS), jnp.int32)
+        end = jnp.int32(0)
+        for k in range(DOCS):
+            end = end + lengths[k, dp]
+            row_doc = row_doc + (row_pos >= end).astype(jnp.int32)
+            col_doc = col_doc + (col_pos >= end).astype(jnp.int32)
+        bias[...] = jnp.where((row_doc == col_doc) & (col_pos <= row_pos), 0.0, NEGATIVE)
+
     def in_range(g):
         return (g >= 0) & (g < GROUPS)
 
     def tick(index, _):
         t = index + FIRST_TICK
+
+        @pl.when(t == -1)
+        def _():
+            prepare()
 
         @pl.when(t == 0)
         def _():

time: 87.6 us -> 87.6 us (level)
  no operation moved by 1% of the time
where the time goes in v3:
time: 87.6 us; the launch traced here: 87.5 us
  Pallas kernels  86.8 us (99%)
    pallas_call x1, Pallas kernels, body(): pl.pallas_call(kernel, out_shape=(rows, rows, gathered), in_specs=[hbm] *...  84.5 us
    pallas_call x1, Pallas kernels, body(): pl.pallas_call(store, out_shape=(wide, wide, narrow, narrow), in_specs=[p...  2.3 us

profile of v3, /device:TPU:6, one launch (start us, length us, event | category | flops | bytes accessed | tf_op | source)
XLA Modules:
  0.0 87.5 jit_solution(10796002562212377899)
XLA Ops:
  0.6 84.5 %shard_map.84 = (bf16[128,8192]{1,0:T(8,128)(2,1)S(1)}, bf16[128,8192]{1,0:T(8,128)(2,1)S(1)}, bf16[8,2,128,128]{3,2,1,0:T(8,128)(2,1)S(1)}) custom-call(bf16[128,8192]{1,0:T(8,128)(2,1)} %query_hbm.1, bf16[128,1024]{1,0:T(8,128)(2,1)} %key_hbm.1, bf16[128,1024]{1,0:T(8,128)(2,1)} %value_hbm.1, bf16[128,8192]{1,0:T(8,128)(2,1)} %grad_hbm.1, s32[8,32]{1,0:T(8,128)} %bitcast.1), custom_call_target="tpu_custom_call" | custom-call | tf_op jit(solution)/shard_map/pallas_call | solution.py:318
  85.2 2.3 %shard_map.85 = (bf16[128,8192]{1,0:T(8,128)(2,1)}, bf16[128,8192]{1,0:T(8,128)(2,1)}, bf16[128,1024]{1,0:T(8,128)(2,1)}, bf16[128,1024]{1,0:T(8,128)(2,1)}) custom-call(bf16[128,8192]{1,0:T(8,128)(2,1)S(1)} %get-tuple-element.7.out, bf16[128,8192]{1,0:T(8,128)(2,1)S(1)} %get-tuple-element.8.dquery, bf16[8,2,128,128]{3,2,1,0:T(8,128)(2,1)S(1)} %get-tuple-element.9.dkv), custom_call_target="tpu_custom_call" | custom-call | tf_op jit(solution)/shard_map/pallas_call | solution.py:336
